TPU v7x, 32 devices: a whole 2x2x4 slice. The times are simulated.
32 devices in a mesh: fsdp: 4 (over y, x), ctx: 8 (over z, core).
Axes of the slice: x: 2, y: 2, z: 4, core: 2. Of those that a mesh axis runs over, the one named last changes fastest.
Arguments:
- tokens: bfloat16 [8192, 768], P(('fsdp', 'ctx')), may hold values from -6 to 6
- cotangent: bfloat16 [8192, 768], P(('fsdp', 'ctx')), may hold values from -6 to 6
- lengths: int32 [4], P('fsdp'), may hold values from 256 to 2048, as said below
- block_table: int32 [16], replicated, may hold values from 0 to 15, each once
- qkv_weight: bfloat16 [768, 2304], P('fsdp'), may hold values from -0.21875 to 0.21875
- query_bias: bfloat16 [768], P('fsdp'), may hold values from -3 to 3
- value_bias: bfloat16 [768], P('fsdp'), may hold values from -0.039794922 to 0.039794922
- proj_weight: bfloat16 [768, 768], P('fsdp')
- proj_bias: bfloat16 [768], P('fsdp'), may hold values from -3 to 3
- gain_first: bfloat16 [768], P('fsdp'), may hold values from 0.5 to 1.5
- shift_first: bfloat16 [768], P('fsdp'), may hold values from -3 to 3
- inner_weight: bfloat16 [768, 3072], P('fsdp'), may hold values from -0.21875 to 0.21875
- inner_bias: bfloat16 [3072], P('fsdp'), may hold values from -3 to 3
- outer_weight: bfloat16 [3072, 768], P('fsdp'), may hold values from -0.109375 to 0.109375
- outer_bias: bfloat16 [768], P('fsdp'), may hold values from -3 to 3
- gain_second: bfloat16 [768], P('fsdp'), may hold values from 0.5 to 1.5
- shift_second: bfloat16 [768], P('fsdp'), may hold values from -3 to 3
Outputs:
- layer_out: bfloat16 [8192, 768], P(('fsdp', 'ctx'))
- tokens_grad: bfloat16 [8192, 768], P(('fsdp', 'ctx'))
- qkv_weight_grad: float32 [768, 2304], P('fsdp')
- query_bias_grad: float32 [768], P('fsdp')
- value_bias_grad: float32 [768], P('fsdp')
- proj_weight_grad: float32 [768, 768], P('fsdp')
- proj_bias_grad: float32 [768], P('fsdp')
- gain_first_grad: float32 [768], P('fsdp')
- shift_first_grad: float32 [768], P('fsdp')
- inner_weight_grad: float32 [768, 3072], P('fsdp')
- inner_bias_grad: float32 [3072], P('fsdp')
- outer_weight_grad: float32 [3072, 768], P('fsdp')
- outer_bias_grad: float32 [768], P('fsdp')
- gain_second_grad: float32 [768], P('fsdp')
- shift_second_grad: float32 [768], P('fsdp')
Inputs may be any that keep to these rules, and one draw needn't show every extreme that they name: `lengths`: one sequence is full. `block_table`: each value appears once.
All inputs are finite; a program needn't handle non-finite values.
Results may differ from a plain program's by a relative error of at most 0.02.
Values may be sent and summed in bfloat16 or wider, within the bound.
A program may use at most 320 MiB of HBM per device.

v0:
```python
import math
import jax
import jax.numpy as jnp
from jax import lax
from jax.sharding import PartitionSpec as P

HEADS = 12
HEAD_DIM = 64
BLK = 128
NEG_FILL = -1e30
NORM_EPS = 1e-05


def layer_norm(vector_in, gain_in, shift_in):
    center = vector_in - jnp.mean(vector_in, axis=-1, keepdims=True)
    spread = jnp.mean(center * center, axis=-1, keepdims=True)
    return center * lax.rsqrt(spread + NORM_EPS) * gain_in + shift_in


def gelu_exact(vector_in):
    return jax.nn.gelu(vector_in, approximate=False)


def cross_dot(first_op, second_op):
    return lax.dot_general(
        first_op, second_op, (((0,), (0,)), ((), ())), preferred_element_type=jnp.float32
    )


def back_dot(first_op, second_op):
    return lax.dot_general(
        first_op, second_op, (((1,), (1,)), ((), ())), preferred_element_type=jnp.float32
    )


def key_valid(start_row, piece_rows, blk_rows, block_table, seq_length):
    index_rows = start_row + jnp.arange(piece_rows, dtype=jnp.int32)
    owner_block = index_rows // blk_rows
    table_slots = jnp.arange(block_table.shape[0], dtype=jnp.int32)
    placed = jnp.sum(
        jnp.where(owner_block[:, None] == table_slots[None, :], block_table[None, :], 0), axis=1
    )
    return placed * blk_rows + index_rows % blk_rows < seq_length


def exp_scores(query_blk, key_blk, valid_keys, lse_blk, score_scale):
    scores = (
        jnp.einsum("qhd,khd->hqk", query_blk, key_blk, preferred_element_type=jnp.float32)
        * score_scale
    )
    scores = jnp.where(valid_keys[None, None, :], scores, NEG_FILL)
    return jnp.exp(scores - lse_blk[:, :, None])


def local(
    tokens,
    cotangent,
    lengths,
    block_table,
    qkv_weight,
    query_bias,
    value_bias,
    proj_weight,
    proj_bias,
    gain_first,
    shift_first,
    inner_weight,
    inner_bias,
    outer_weight,
    outer_bias,
    gain_second,
    shift_second,
):
    feat_width = HEADS * HEAD_DIM
    tok_rows = tokens.shape[0]
    blk_rows = BLK
    score_scale = 1.0 / math.sqrt(HEAD_DIM)
    seq_length = lengths[0]
    qkv_full, qbias_full, vbias_full, proj_full, pbias_full, gain1_full, shift1_full = (
        lax.all_gather(qkv_weight, "fsdp", axis=0, tiled=True),
        lax.all_gather(query_bias, "fsdp", axis=0, tiled=True),
        lax.all_gather(value_bias, "fsdp", axis=0, tiled=True),
        lax.all_gather(proj_weight, "fsdp", axis=0, tiled=True),
        lax.all_gather(proj_bias, "fsdp", axis=0, tiled=True),
        lax.all_gather(gain_first, "fsdp", axis=0, tiled=True),
        lax.all_gather(shift_first, "fsdp", axis=0, tiled=True),
    )
    inner_full, ibias_full, outer_full, obias_full, gain2_full, shift2_full = (
        lax.all_gather(inner_weight, "fsdp", axis=0, tiled=True),
        lax.all_gather(inner_bias, "fsdp", axis=0, tiled=True),
        lax.all_gather(outer_weight, "fsdp", axis=0, tiled=True),
        lax.all_gather(outer_bias, "fsdp", axis=0, tiled=True),
        lax.all_gather(gain_second, "fsdp", axis=0, tiled=True),
        lax.all_gather(shift_second, "fsdp", axis=0, tiled=True),
    )
    tokens_wide = tokens.astype(jnp.float32)
    bias_row = jnp.concatenate([qbias_full, jnp.zeros_like(qbias_full), vbias_full]).astype(
        jnp.float32
    )
    packed = (jnp.dot(tokens, qkv_full, preferred_element_type=jnp.float32) + bias_row).astype(
        jnp.bfloat16
    )
    queries = packed[:, :feat_width]
    key_rows = packed[:, feat_width : 2 * feat_width]
    value_rows = packed[:, 2 * feat_width :]
    query_heads = queries.reshape(tok_rows, HEADS, HEAD_DIM)
    start_state = (
        jnp.full((HEADS, tok_rows), NEG_FILL, jnp.float32),
        jnp.zeros((HEADS, tok_rows), jnp.float32),
        jnp.zeros((tok_rows, HEADS, HEAD_DIM), jnp.float32),
    )
    key_piece = lax.all_gather(key_rows, "ctx", axis=0, tiled=True)
    value_piece = lax.all_gather(value_rows, "ctx", axis=0, tiled=True)
    piece_rows = key_piece.shape[0]
    fold_blk_size = math.gcd(piece_rows, 1024)
    num_blocks = piece_rows // fold_blk_size
    key_blocks = key_piece.reshape(num_blocks, fold_blk_size, HEADS, HEAD_DIM)
    value_blocks = value_piece.reshape(num_blocks, fold_blk_size, HEADS, HEAD_DIM)
    offsets = fold_blk_size * jnp.arange(num_blocks, dtype=jnp.int32)

    def scan_step(state_in, loop_item):
        running_max, running_sum, accum_out = state_in
        key_blk, value_blk, offset = loop_item
        valid_keys = key_valid(offset, fold_blk_size, blk_rows, block_table, seq_length)
        scores = (
            jnp.einsum("qhd,khd->hqk", query_heads, key_blk, preferred_element_type=jnp.float32)
            * score_scale
        )
        scores = jnp.where(valid_keys[None, None, :], scores, NEG_FILL)
        new_max = jnp.maximum(running_max, jnp.max(scores, axis=2))
        factor = jnp.exp(running_max - new_max)
        soft_weights = jnp.exp(scores - new_max[:, :, None])
        new_sum = running_sum * factor + jnp.sum(soft_weights, axis=2)
        update = jnp.einsum(
            "hqk,khd->qhd",
            soft_weights.astype(jnp.bfloat16),
            value_blk,
            preferred_element_type=jnp.float32,
        )
        accum_out = accum_out * jnp.transpose(factor)[:, :, None] + update
        return ((new_max, new_sum, accum_out), None)

    result, _ = lax.scan(scan_step, start_state, (key_blocks, value_blocks, offsets))
    run_max, run_sum, accum_out = result
    lse = run_max + jnp.log(run_sum)
    attn_heads = accum_out / jnp.transpose(run_sum)[:, :, None]
    context = attn_heads.reshape(tok_rows, feat_width).astype(jnp.bfloat16)
    hidden = (
        tokens_wide
        + jnp.dot(context, proj_full, preferred_element_type=jnp.float32)
        + pbias_full.astype(jnp.float32)
    )
    normed, norm_back = jax.vjp(
        layer_norm, hidden, gain1_full.astype(jnp.float32), shift1_full.astype(jnp.float32)
    )
    normed_low = normed.astype(jnp.bfloat16)
    inner_pre = jnp.dot(
        normed_low, inner_full, preferred_element_type=jnp.float32
    ) + ibias_full.astype(jnp.float32)
    active, gelu_back = jax.vjp(gelu_exact, inner_pre)
    active_low = active.astype(jnp.bfloat16)
    mixed_sum = (
        normed
        + jnp.dot(active_low, outer_full, preferred_element_type=jnp.float32)
        + obias_full.astype(jnp.float32)
    )
    result, final_back = jax.vjp(
        layer_norm, mixed_sum, gain2_full.astype(jnp.float32), shift2_full.astype(jnp.float32)
    )
    layer_out = result.astype(jnp.bfloat16)
    mixed_grad, gain2_grad, shift2_grad = final_back(cotangent.astype(jnp.float32))
    branch_low = mixed_grad.astype(jnp.bfloat16)
    outer_grad = cross_dot(active_low, branch_low)
    obias_grad = jnp.sum(branch_low.astype(jnp.float32), axis=0)
    (inner_grad_wide,) = gelu_back(back_dot(branch_low, outer_full))
    inner_low = inner_grad_wide.astype(jnp.bfloat16)
    inner_grad = cross_dot(normed_low, inner_low)
    ibias_grad = jnp.sum(inner_low.astype(jnp.float32), axis=0)
    normed_grad = mixed_grad + back_dot(inner_low, inner_full)
    hidden_grad, gain1_grad, shift1_grad = norm_back(normed_grad)
    proj_low = hidden_grad.astype(jnp.bfloat16)
    proj_grad = cross_dot(context, proj_low)
    pbias_grad = jnp.sum(proj_low.astype(jnp.float32), axis=0)
    context_grad = back_dot(proj_low, proj_full).astype(jnp.bfloat16)
    grad_heads = context_grad.reshape(tok_rows, HEADS, HEAD_DIM)
    delta = jnp.einsum("qhd,qhd->hq", grad_heads.astype(jnp.float32), attn_heads)
    gathered_keys, gathered_values = (
        lax.all_gather(key_rows, "ctx", axis=0, tiled=True),
        lax.all_gather(value_rows, "ctx", axis=0, tiled=True),
    )
    total_rows = gathered_keys.shape[0]
    blk_size = math.gcd(total_rows, 1024)
    num_blocks = total_rows // blk_size
    key_blocks = gathered_keys.reshape(num_blocks, blk_size, HEADS, HEAD_DIM)
    value_blocks = gathered_values.reshape(num_blocks, blk_size, HEADS, HEAD_DIM)
    offsets = blk_size * jnp.arange(num_blocks, dtype=jnp.int32)

    def scan_back(query_acc, loop_item):
        key_blk, value_blk, offset = loop_item
        valid_keys = key_valid(offset, blk_size, blk_rows, block_table, seq_length)
        attn_probs = exp_scores(query_heads, key_blk, valid_keys, lse, score_scale)
        value_part = jnp.einsum(
            "hqk,qhd->khd",
            attn_probs.astype(jnp.bfloat16),
            grad_heads,
            preferred_element_type=jnp.float32,
        )
        prob_grad = jnp.einsum(
            "qhd,khd->hqk", grad_heads, value_blk, preferred_element_type=jnp.float32
        )
        score_low = (attn_probs * (prob_grad - delta[:, :, None])).astype(jnp.bfloat16)
        query_acc = (
            query_acc
            + jnp.einsum("hqk,khd->qhd", score_low, key_blk, preferred_element_type=jnp.float32)
            * score_scale
        )
        key_part = (
            jnp.einsum("hqk,qhd->khd", score_low, query_heads, preferred_element_type=jnp.float32)
            * score_scale
        )
        return (
            query_acc,
            jnp.concatenate(
                [key_part.reshape(blk_size, feat_width), value_part.reshape(blk_size, feat_width)],
                axis=1,
            ),
        )

    query_acc, terms = lax.scan(
        scan_back,
        jnp.zeros((tok_rows, HEADS, HEAD_DIM), jnp.float32),
        (key_blocks, value_blocks, offsets),
    )
    key_value_grad = lax.psum_scatter(
        terms.reshape(total_rows, 2 * feat_width), "ctx", scatter_dimension=0, tiled=True
    )
    query_grad = query_acc.reshape(tok_rows, feat_width)
    key_grad = key_value_grad[:, :feat_width]
    value_grad = key_value_grad[:, feat_width:]
    packed_grad = jnp.concatenate([query_grad, key_grad, value_grad], axis=1).astype(jnp.bfloat16)
    qkv_grad = cross_dot(tokens, packed_grad)
    qbias_grad = jnp.sum(packed_grad[:, :feat_width].astype(jnp.float32), axis=0)
    vbias_grad = jnp.sum(packed_grad[:, 2 * feat_width :].astype(jnp.float32), axis=0)
    tokens_grad = (hidden_grad + back_dot(packed_grad, qkv_full)).astype(jnp.bfloat16)
    qkv_part, qbias_part, vbias_part, proj_part, pbias_part, gain1_part, shift1_part = (
        lax.psum_scatter(
            qkv_grad.astype(jnp.bfloat16), "fsdp", scatter_dimension=0, tiled=True
        ).astype(jnp.float32),
        lax.psum_scatter(
            qbias_grad.astype(jnp.bfloat16), "fsdp", scatter_dimension=0, tiled=True
        ).astype(jnp.float32),
        lax.psum_scatter(
            vbias_grad.astype(jnp.bfloat16), "fsdp", scatter_dimension=0, tiled=True
        ).astype(jnp.float32),
        lax.psum_scatter(
            proj_grad.astype(jnp.bfloat16), "fsdp", scatter_dimension=0, tiled=True
        ).astype(jnp.float32),
        lax.psum_scatter(
            pbias_grad.astype(jnp.bfloat16), "fsdp", scatter_dimension=0, tiled=True
        ).astype(jnp.float32),
        lax.psum_scatter(
            gain1_grad.astype(jnp.bfloat16), "fsdp", scatter_dimension=0, tiled=True
        ).astype(jnp.float32),
        lax.psum_scatter(
            shift1_grad.astype(jnp.bfloat16), "fsdp", scatter_dimension=0, tiled=True
        ).astype(jnp.float32),
    )
    inner_part, ibias_part, outer_part, obias_part, gain2_part, shift2_part = (
        lax.psum_scatter(
            inner_grad.astype(jnp.bfloat16), "fsdp", scatter_dimension=0, tiled=True
        ).astype(jnp.float32),
        lax.psum_scatter(
            ibias_grad.astype(jnp.bfloat16), "fsdp", scatter_dimension=0, tiled=True
        ).astype(jnp.float32),
        lax.psum_scatter(
            outer_grad.astype(jnp.bfloat16), "fsdp", scatter_dimension=0, tiled=True
        ).astype(jnp.float32),
        lax.psum_scatter(
            obias_grad.astype(jnp.bfloat16), "fsdp", scatter_dimension=0, tiled=True
        ).astype(jnp.float32),
        lax.psum_scatter(
            gain2_grad.astype(jnp.bfloat16), "fsdp", scatter_dimension=0, tiled=True
        ).astype(jnp.float32),
        lax.psum_scatter(
            shift2_grad.astype(jnp.bfloat16), "fsdp", scatter_dimension=0, tiled=True
        ).astype(jnp.float32),
    )
    summed = lax.psum(
        (
            qkv_part,
            qbias_part,
            vbias_part,
            proj_part,
            pbias_part,
            gain1_part,
            shift1_part,
            inner_part,
            ibias_part,
            outer_part,
            obias_part,
            gain2_part,
            shift2_part,
        ),
        "ctx",
    )
    return (
        layer_out,
        tokens_grad,
        summed[0],
        summed[1],
        summed[2],
        summed[3],
        summed[4],
        summed[5],
        summed[6],
        summed[7],
        summed[8],
        summed[9],
        summed[10],
        summed[11],
        summed[12],
    )


def solution(mesh):
    placed = (
        P(("fsdp", "ctx"), None),
        P(("fsdp", "ctx"), None),
        P("fsdp"),
        P(),
        P("fsdp", None),
        P("fsdp"),
        P("fsdp"),
        P("fsdp", None),
        P("fsdp"),
        P("fsdp"),
        P("fsdp"),
        P("fsdp", None),
        P("fsdp"),
        P("fsdp", None),
        P("fsdp"),
        P("fsdp"),
        P("fsdp"),
    )
    return jax.shard_map(
        local,
        mesh=mesh,
        in_specs=placed,
        out_specs=(
            P(("fsdp", "ctx"), None),
            P(("fsdp", "ctx"), None),
            P("fsdp", None),
            P("fsdp"),
            P("fsdp"),
            P("fsdp", None),
            P("fsdp"),
            P("fsdp"),
            P("fsdp"),
            P("fsdp", None),
            P("fsdp"),
            P("fsdp", None),
            P("fsdp"),
            P("fsdp"),
            P("fsdp"),
        ),
        check_vma=False,
    )
```

profile of v0, /device:TPU:0, one launch (start us, length us, event | category | flops | bytes accessed | tf_op | source)
XLA Modules:
  0.0 886.6 jit_solution(12183889524991659899)
XLA Ops:
  15.8 17.8 %all-reduce.19 = (bf16[768]{0:T(1024)(128)(2,1)S(1)}, bf16[768]{0:T(1024)(128)(2,1)S(1)}, bf16[768]{0:T(1024)(128)(2,1)S(1)}, bf16[768]{0:T(1024)(128)(2,1)S(1)}...) all-reduce(bf16[768]{0:T(1024)(128)(2,1)S(1)} %dynamic-update-slice, ...), channel_id=1, replica_groups=mesh['fsdp'=4,'ctx'=8] {'fsdp'}, use_global_device_ids=true, to_apply=%add.1 | all-reduce | flops 5376 | bytes 21504
  33.7 26.3 %all-gather.8.cloned.1.call-done = bf16[768,2304]{1,0:T(8,128)(2,1)} async-done(((bf16[192,2304]{1,0:T(8,128)(2,1)}), bf16[768,2304]{1,0:T(8,128)(2,1)}) %all-gather.8.cloned.1.call-update) | async-done | bytes 3538960 | tf_op jit(solution)/shard_map/all_gather | solution.py:80
  60.0 3.2 fusion.68
  67.9 8.4 all-gather
  79.4 23.2 %all-gather.10.cloned.1.call-done = bf16[2048,768]{1,0:T(8,128)(2,1)} async-done(((bf16[256,768]{1,0:T(8,128)(2,1)}), bf16[2048,768]{1,0:T(8,128)(2,1)}) %all-gather.10.cloned.1.call-update) | async-done | bytes 3145744 | tf_op jit(solution)/shard_map/all_gather | solution.py:112
  102.6 3.2 copy.79
  105.8 4.0 reshape.228
  109.8 3.1 copy.82
  112.9 29.1 %all-gather.12.cloned.1.call-done = bf16[2048,768]{1,0:T(8,128)(2,1)} async-done(((bf16[256,768]{1,0:T(8,128)(2,1)}), bf16[2048,768]{1,0:T(8,128)(2,1)}) %all-gather.12.cloned.1.call-update) | async-done | bytes 3145744 | tf_op jit(solution)/shard_map/all_gather | solution.py:113
  142.0 4.7 copy.81
  146.7 6.2 reshape.230
  152.9 4.5 copy.83
  157.4 50.1 %while.32 = (s32[]{:T(128)}, f32[12,256]{1,0:T(8,128)S(1)}, f32[12,256]{1,0:T(8,128)}, f32[256,12,64]{0,2,1:T(8,128)}, s32[2]{0:T(128)}, /*index=5*/s32[16]{0:T(...) while((s32[]{:T(128)}, f32[12,256]{1,0:T(8,128)S(1)}, ...), condition=%wide.region_4.5_spmd.clone, body=%wide.region_0.4_spmd.clone.sunk | while | flops 840597504 | bytes 93516152 | solution.py:143
  161.4 6.7 bitcast_reduce_fusion.2
  168.9 7.4 fusion.156
  177.1 5.1 fusion.158
  186.2 6.7 bitcast_reduce_fusion.2
  193.7 7.4 fusion.156
  202.2 5.3 fusion.158
  207.5 2.0 fusion.84
  209.5 2.1 fusion.100
  213.9 15.3 %all-gather.16.cloned.1.call-done = bf16[768,3072]{1,0:T(8,128)(2,1)} async-done(((bf16[192,3072]{1,0:T(8,128)(2,1)}), bf16[768,3072]{1,0:T(8,128)(2,1)}) %all-gather.16.cloned.1.call-update) | async-done | bytes 4718608 | tf_op jit(solution)/shard_map/all_gather | solution.py:89
  229.2 12.7 %multiply_convert_fusion.1 = (bf16[256,3072]{1,0:T(8,128)(2,1)}, f32[256,3072]{1,0:T(8,128)}, f32[256,3072]{1,0:T(8,128)}) fusion(f32[3072]{0:T(1024)} %bitcast.169, bf16[768,3072]{1,0:T(8,128)(2,1)} %all-gather.16.cloned.1.call-done, f32[256,768]{1,0:T(8,128)} %copy-done.3, f32[768]{0:T(1024)} %convert_element_type.168, f32[768]{0:T(1024)} %convert_element_type.167, ...), kind=kOutput, calls=%fused_computation.91 | convolution fusion | flops 1260847104 | bytes 13389824 | tf_op jit(solution)/shard_map/dot_general | solution.py:157
  241.9 46.0 %all-gather.18.cloned.1.call-done = bf16[3072,768]{1,0:T(8,128)(2,1)} async-done(((bf16[768,768]{1,0:T(8,128)(2,1)}), bf16[3072,768]{1,0:T(8,128)(2,1)}) %all-gather.18.cloned.1.call-update) | async-done | bytes 4718608 | tf_op jit(solution)/shard_map/all_gather | solution.py:91
  288.0 4.7 fusion.101
  295.1 2.8 fusion.92
  298.0 2.4 multiply_reduce_fusion
  304.4 1.9 copy.84
  306.3 2.0 fusion.82
  308.3 81.3 %while.33 = (s32[]{:T(128)}, f32[256,12,64]{0,2,1:T(8,128)}, f32[2,1024,1536]{2,1,0:T(8,128)}, bf16[2,1024,12,64]{1,3,2,0:T(8,128)(2,1)S(1)}, s32[2]{0:T(128)}, ...) while((s32[]{:T(128)}, f32[256,12,64]{0,2,1:T(8,128)}, ...), condition=%wide.region_15.16_spmd.clone, body=%wide.region_13.15_spmd.clone.sunk | while | flops 2047752192 | bytes 193675104 | solution.py:229
  308.5 1.8 fusion.169
  311.8 1.4 fusion.170
  313.3 6.4 multiply_convert_fusion.3
  319.7 5.0 fusion.171
  324.7 6.5 fusion.172
  331.2 2.0 convolution_multiply_fusion.2
  333.2 3.2 maximum_bitcast_fusion.2
  336.4 6.6 copy.116
  343.0 5.9 constant_dynamic-update-slice_fusion.2
  349.0 1.8 fusion.169
  353.7 6.4 multiply_convert_fusion.3
  360.2 5.1 fusion.171
  365.3 6.5 fusion.172
  371.8 2.0 convolution_multiply_fusion.2
  373.8 3.2 maximum_bitcast_fusion.2
  377.1 6.6 copy.116
  383.6 5.9 constant_dynamic-update-slice_fusion.2
  390.7 1.5 convolution_convert_fusion.3
  392.3 3.9 convolution_convert_fusion.1
  396.5 1.5 copy-done.12
  398.0 3.6 convolution_convert_fusion
  403.9 115.1 %reduce-scatter.8.cloned.1.call-done = f32[256,1536]{1,0:T(8,128)} async-done(((f32[2048,1536]{1,0:T(8,128)}), f32[256,1536]{1,0:T(8,128)}) %reduce-scatter.8.cloned.1.call-update) | async-done | bytes 1572880 | tf_op jit(solution)/shard_map/reduce_scatter | solution.py:234
  519.0 1.5 convert.14
  521.3 2.2 fusion.67
  523.6 3.9 copy.99
  530.2 19.1 %reduce-scatter.10.cloned.1.call-done = bf16[192,768]{1,0:T(8,128)(2,1)} async-done(((bf16[768,768]{1,0:T(8,128)(2,1)}), bf16[192,768]{1,0:T(8,128)(2,1)}) %reduce-scatter.10.cloned.1.call-update) | async-done | bytes 294928 | tf_op jit(solution)/shard_map/reduce_scatter | solution.py:255
  549.4 60.1 %reduce-scatter.12.cloned.1.call-done = bf16[192,3072]{1,0:T(8,128)(2,1)} async-done(((bf16[768,3072]{1,0:T(8,128)(2,1)}), bf16[192,3072]{1,0:T(8,128)(2,1)}) %reduce-scatter.12.cloned.1.call-update) | async-done | bytes 1179664 | tf_op jit(solution)/shard_map/reduce_scatter | solution.py:269
  609.5 60.0 %reduce-scatter.14.cloned.1.call-done = bf16[768,768]{1,0:T(8,128)(2,1)} async-done(((bf16[3072,768]{1,0:T(8,128)(2,1)}), bf16[768,768]{1,0:T(8,128)(2,1)}) %reduce-scatter.14.cloned.1.call-update) | async-done | bytes 1179664 | tf_op jit(solution)/shard_map/reduce_scatter | solution.py:275
  669.6 15.5 %all-reduce.18 = (bf16[768]{0:T(1024)(128)(2,1)S(1)}, bf16[768]{0:T(1024)(128)(2,1)S(1)}, bf16[768]{0:T(1024)(128)(2,1)S(1)}, bf16[768]{0:T(1024)(128)(2,1)S(1)}...) all-reduce(bf16[768]{0:T(1024)(128)(2,1)S(1)} %dynamic-update-slice, ...), channel_id=1, replica_groups=mesh['fsdp'=4,'ctx'=8] {'fsdp'}, use_global_device_ids=true, to_apply=%add.7 | all-reduce | flops 9984 | bytes 39936
  688.2 3.9 fusion.77
  692.1 27.9 %reduce-scatter.16.cloned.1.call-done = bf16[192,2304]{1,0:T(8,128)(2,1)} async-done(((bf16[768,2304]{1,0:T(8,128)(2,1)}), bf16[192,2304]{1,0:T(8,128)(2,1)}) %reduce-scatter.16.cloned.1.call-update) | async-done | bytes 884752
  720.0 1.5 copy.100
  721.5 156.5 %all-reduce.21 = (f32[192,2304]{0,1:T(8,128)S(1)}, f32[192]{0:T(256)}, f32[192]{0:T(256)}, f32[192,768]{1,0:T(8,128)}, f32[192]{0:T(256)}, /*index=5*/f32[192]{0...) all-reduce(bf16[192,2304]{0,1:T(8,128)(2,1)S(1)} %copy.100, ...), channel_id=1, replica_groups=mesh['fsdp'=4,'ctx'=8] {'ctx'}, use_global_device_ids=true, to_apply=%region_18.19 | all-reduce | flops 1771776 | bytes 10635264 | tf_op jit(solution)/shard_map/psum | solution.py:288
  878.0 1.8 copy.89
  (294 shorter events, 49.0 us)
Async XLA Ops:
  7.2 52.8 %all-gather.8.cloned.1.call-start = ((), (), s32[]{:S(2)}) async-start(), calls=%async_computation.5 | async-start | bytes 4423680 | tf_op jit(solution)/shard_map/all_gather | solution.py:80
  7.9 94.7 %all-gather.10.cloned.1.call-start = ((), (), s32[]{:S(2)}) async-start(), calls=%async_computation.6 | async-start | bytes 3538944 | tf_op jit(solution)/shard_map/all_gather | solution.py:112
  64.2 77.8 %all-gather.12.cloned.1.call-start = ((), (), s32[]{:S(2)}) async-start(), calls=%async_computation.7 | async-start | bytes 3538944 | tf_op jit(solution)/shard_map/all_gather | solution.py:113
  64.9 144.5 %all-gather.14.cloned.1.call-start = ((), (), s32[]{:S(2)}) async-start(), calls=%async_computation.8 | async-start | bytes 1474560 | tf_op jit(solution)/shard_map/all_gather | solution.py:83
  65.5 163.6 %all-gather.16.cloned.1.call-start = ((), (), s32[]{:S(2)}) async-start(), calls=%async_computation.9 | async-start | bytes 5898240 | tf_op jit(solution)/shard_map/all_gather | solution.py:89
  66.1 221.8 %all-gather.18.cloned.1.call-start = ((), (), s32[]{:S(2)}) async-start(), calls=%async_computation.10 | async-start | bytes 5898240 | tf_op jit(solution)/shard_map/all_gather | solution.py:91
  66.7 452.3 %reduce-scatter.8.cloned.1.call-start = ((), (), s32[]{:S(2)}) async-start(), calls=%async_computation.11 | async-start | bytes 14155776 | tf_op jit(solution)/shard_map/reduce_scatter | solution.py:234
  161.4 6.7 copy-start.31
  168.9 7.4 copy-start.26
  168.9 8.2 copy-start
  168.9 8.2 copy-start.32
  176.3 6.0 copy-start.27
  186.2 6.7 copy-start.31
  193.7 7.4 copy-start.26
  193.7 8.5 copy-start
  193.7 8.5 copy-start.32
  201.1 6.4 copy-start.27
  229.1 58.8 %copy-start.33 = (f32[768]{0:T(1024)S(1)}, f32[768]{0:T(1024)}, u32[]{:S(2)}) copy-start(f32[768]{0:T(1024)} %convert_element_type.167) | copy-start | bytes 9220
  229.1 58.8 %copy-start.36 = (f32[768]{0:T(1024)S(1)}, f32[768]{0:T(1024)}, u32[]{:S(2)}) copy-start(f32[768]{0:T(1024)} %convert_element_type.168) | copy-start | bytes 9220
  229.1 58.8 %copy-start.44 = (f32[256]{0:T(256)S(1)}, f32[256]{0:T(256)}, u32[]{:S(2)}) copy-start(f32[256]{0:T(256)} %copy-done.43) | copy-start | bytes 3076
  229.1 58.8 %copy-start.52 = (f32[256]{0:T(256)S(1)}, f32[256]{0:T(256)}, u32[]{:S(2)}) copy-start(f32[256]{0:T(256)} %fusion.85) | copy-start | bytes 3076
  287.9 7.1 slice-start.4
  288.0 5.0 copy-start.10
  288.0 5.0 copy-start.38
  288.0 7.1 slice-start.5
  288.0 7.1 copy-start.69
  293.0 4.9 copy-start.50
  300.4 5.9 copy-start.29
  308.4 4.8 copy-start.15
  308.5 4.8 copy-start.22
  308.5 4.8 copy-start.47
  308.5 4.8 copy-start.48
  310.3 9.3 %copy-start.1 = (f32[12,1024,256]{2,1,0:T(8,128)}, f32[12,1024,256]{2,1,0:T(8,128)S(1)}, u32[]{:S(2)}) copy-start(f32[12,1024,256]{2,1,0:T(8,128)S(1)} %fusion.169) | copy-start | bytes 37748740 | tf_op jit(solution)/shard_map/while
  319.7 5.0 copy-start.23
  319.7 5.0 copy-start.49
  319.7 11.5 %slice-start = ((s8[6291456]{0:T(1024)(128)(4,1)}), s8[4194304]{0:T(1024)(128)(4,1)S(1)}, s32[]{:S(2)}) async-start(s8[6291456]{0:T(1024)(128)(4,1)} %bitcast.156), calls=%async_computation.16 | async-start | bytes 8388608 | tf_op jit(solution)/shard_map/while
  324.7 6.5 slice-start.1
  348.9 4.8 copy-start.15
  348.9 4.8 copy-start.22
  348.9 4.8 copy-start.47
  349.0 4.8 copy-start.48
  350.8 9.3 %copy-start.1 = (f32[12,1024,256]{2,1,0:T(8,128)}, f32[12,1024,256]{2,1,0:T(8,128)S(1)}, u32[]{:S(2)}) copy-start(f32[12,1024,256]{2,1,0:T(8,128)S(1)} %fusion.169) | copy-start | bytes 37748740 | tf_op jit(solution)/shard_map/while
  360.2 5.1 copy-start.23
  360.2 5.1 copy-start.49
  360.2 11.7 %slice-start = ((s8[6291456]{0:T(1024)(128)(4,1)}), s8[4194304]{0:T(1024)(128)(4,1)S(1)}, s32[]{:S(2)}) async-start(s8[6291456]{0:T(1024)(128)(4,1)} %bitcast.156), calls=%async_computation.16 | async-start | bytes 8388608 | tf_op jit(solution)/shard_map/while
  365.3 6.5 slice-start.1
  389.6 159.7 %reduce-scatter.10.cloned.1.call-start = ((), (), s32[]{:S(2)}) async-start(), calls=%async_computation.12 | async-start | bytes 1474560 | tf_op jit(solution)/shard_map/reduce_scatter | solution.py:255
  392.2 217.3 %reduce-scatter.12.cloned.1.call-start = ((), (), s32[]{:S(2)}) async-start(), calls=%async_computation.13 | async-start | bytes 5898240 | tf_op jit(solution)/shard_map/reduce_scatter | solution.py:269
  396.2 273.2 %reduce-scatter.14.cloned.1.call-start = ((), (), s32[]{:S(2)}) async-start(), calls=%async_computation.14 | async-start | bytes 5898240 | tf_op jit(solution)/shard_map/reduce_scatter | solution.py:275
  401.7 318.3 %reduce-scatter.16.cloned.1.call-start = ((), (), s32[]{:S(2)}) async-start(), calls=%async_computation.15 | async-start | bytes 4423680
  527.5 141.9 %copy-start.19 = (bf16[256,1536]{1,0:T(8,128)(2,1)S(1)}, bf16[256,1536]{1,0:T(8,128)(2,1)}, u32[]{:S(2)}) copy-start(bf16[256,1536]{1,0:T(8,128)(2,1)} %copy-done.18) | copy-start | bytes 2359300
  527.5 142.0 %copy-start.57 = (bf16[768]{0:T(1024)(128)(2,1)S(1)}, bf16[768]{0:T(1024)(128)(2,1)}, u32[]{:S(2)}) copy-start(bf16[768]{0:T(1024)(128)(2,1)} %get-tuple-element.562) | copy-start | bytes 4612
  527.5 142.0 %copy-start.58 = (bf16[768]{0:T(1024)(128)(2,1)S(1)}, bf16[768]{0:T(1024)(128)(2,1)}, u32[]{:S(2)}) copy-start(bf16[768]{0:T(1024)(128)(2,1)} %get-tuple-element.641) | copy-start | bytes 4612
  527.5 142.0 %copy-start.59 = (bf16[768]{0:T(1024)(128)(2,1)S(1)}, bf16[768]{0:T(1024)(128)(2,1)}, u32[]{:S(2)}) copy-start(bf16[768]{0:T(1024)(128)(2,1)} %get-tuple-element.645) | copy-start | bytes 4612
  527.5 142.0 %copy-start.60 = (bf16[3072]{0:T(1024)(128)(2,1)S(1)}, bf16[3072]{0:T(1024)(128)(2,1)}, u32[]{:S(2)}) copy-start(bf16[3072]{0:T(1024)(128)(2,1)} %get-tuple-element.643) | copy-start | bytes 18436
  527.6 142.0 %copy-start.63 = (bf16[768]{0:T(1024)(128)(2,1)S(1)}, bf16[768]{0:T(1024)(128)(2,1)}, u32[]{:S(2)}) copy-start(bf16[768]{0:T(1024)(128)(2,1)} %get-tuple-element.560) | copy-start | bytes 4612
  527.6 142.0 %copy-start.64 = (bf16[768]{0:T(1024)(128)(2,1)S(1)}, bf16[768]{0:T(1024)(128)(2,1)}, u32[]{:S(2)}) copy-start(bf16[768]{0:T(1024)(128)(2,1)} %get-tuple-element.564) | copy-start | bytes 4612
  527.6 159.6 %copy-start.7 = (f32[256,768]{1,0:T(8,128)S(1)}, f32[256,768]{1,0:T(8,128)}, u32[]{:S(2)}) copy-start(f32[256,768]{1,0:T(8,128)} %copy-done.6) | copy-start | bytes 2359300
  527.6 159.6 %copy-start.39 = (f32[768]{0:T(1024)S(1)}, f32[768]{0:T(1024)}, u32[]{:S(2)}) copy-start(f32[768]{0:T(1024)} %convert_element_type.173) | copy-start | bytes 9220
  527.6 159.6 %copy-start.42 = (f32[256]{0:T(256)S(1)}, f32[256]{0:T(256)}, u32[]{:S(2)}) copy-start(f32[256]{0:T(256)} %copy-done.41) | copy-start | bytes 3076
  527.6 159.6 %copy-start.51 = (f32[256]{0:T(256)S(1)}, f32[256]{0:T(256)}, u32[]{:S(2)}) copy-start(f32[256]{0:T(256)} %copy-done.50) | copy-start | bytes 3076
  527.6 160.6 %copy-start.17 = (f32[256,768]{1,0:T(8,128)S(1)}, f32[256,768]{1,0:T(8,128)}, u32[]{:S(2)}) copy-start(f32[256,768]{1,0:T(8,128)} %copy-done.16) | copy-start | bytes 2359300
  527.6 160.5 %copy-start.30 = (bf16[256,768]{1,0:T(8,128)(2,1)S(1)}, bf16[256,768]{1,0:T(8,128)(2,1)}, u32[]{:S(2)}) copy-start(bf16[256,768]{1,0:T(8,128)(2,1)} %copy.88) | copy-start | bytes 1179652
  527.6 160.5 %copy-start.62 = (f32[256]{0:T(256)S(1)}, f32[256]{0:T(256)}, u32[]{:S(2)}) copy-start(f32[256]{0:T(256)} %copy-done.61) | copy-start | bytes 3076
  (39 other events, 85.7 us)
Sparse Core Ops, SparseCore 0:
  9.9 50.0 all-gather.7
  64.3 38.2 all-gather.9
  104.9 37.1 all-gather.11
  143.7 26.5 all-gather.13
  172.0 57.0 all-gather.15
  230.8 57.0 all-gather.17
  389.7 129.2 reduce-scatter.7
  522.5 26.8 reduce-scatter.9
  552.4 57.0 reduce-scatter.11
  612.3 57.0 reduce-scatter.13
  672.5 47.4 reduce-scatter.15
where the time goes:
time: 891 us; the launch traced here: 887 us
  waiting for transfers between devices  425 us (48%)
  blocking collectives  198 us (22%)
  matrix products  112 us (13%)
  local copies, waits for them, and re-layouts  83.2 us (9%)
  other arithmetic  50.1 us (6%)
  between operations  16.8 us (2%)
    psum x1, blocking collectives, local(): lax.psum((qkv_part, qbias_part, vbias_part, proj_part, pbias_part, gain1_...  156 us
    reduce_scatter x1, waiting for transfers between devices, local(): lax.psum_scatter(terms.reshape(total_rows, 2 * feat_width), 'ctx', scatte...  115 us
    reduce_scatter x1, waiting for transfers between devices, local(): lax.psum_scatter(inner_grad.astype(jnp.bfloat16), 'fsdp', scatter_dimensi...  60.1 us
    reduce_scatter x1, waiting for transfers between devices, local(): lax.psum_scatter(outer_grad.astype(jnp.bfloat16), 'fsdp', scatter_dimensi...  60 us
    all_gather x1, waiting for transfers between devices, local(): lax.all_gather(outer_weight, 'fsdp', axis=0, tiled=True)  46 us
    unnamed x2, blocking collectives  33.4 us
    unnamed x12, waiting for transfers between devices  31 us
    unnamed x144, local copies, waits for them, and re-layouts  30.2 us
  transfers between devices with their start and end apart: 11, of which 10 were waited for; matrix products, arithmetic and copies ran while one was open for 14% of the time, Pallas kernels for 0%

commit v1 on v0

--- a/solution.py
+++ b/solution.py
@@ -109,8 +109,11 @@
         jnp.zeros((HEADS, tok_rows), jnp.float32),
         jnp.zeros((tok_rows, HEADS, HEAD_DIM), jnp.float32),
     )
-    key_piece = lax.all_gather(key_rows, "ctx", axis=0, tiled=True)
-    value_piece = lax.all_gather(value_rows, "ctx", axis=0, tiled=True)
+    key_piece, value_piece = jnp.split(
+        lax.all_gather(jnp.concatenate([key_rows, value_rows], axis=1), "ctx", axis=0, tiled=True),
+        [key_rows.shape[1]],
+        axis=1,
+    )
     piece_rows = key_piece.shape[0]
     fold_blk_size = math.gcd(piece_rows, 1024)
     num_blocks = piece_rows // fold_blk_size

time: 891 us -> 962 us (1.080)
  local copies, waits for them, and re-layouts: 83.2 us -> 121 us
  waiting for transfers between devices: 425 us -> 447 us
    all_gather x2 -> x3, waiting for transfers between devices: 52.4 us -> 102 us  [the longest x1 50.2 us: local(): lax.all_gather(jnp.concatenate([key_rows, value_rows], axis=1), 'ctx', ax...]
    split x0 -> x3, local copies, waits for them, and re-layouts: none -> 15.4 us  [local(): jnp.split(lax.all_gather(jnp.concatenate([key_rows, value_rows], axis=1),...]
    all_gather x1, waiting for transfers between devices: 15.3 us -> 0.01 us  [local(): lax.all_gather(inner_weight, 'fsdp', axis=0, tiled=True)]
    all_gather x1, waiting for transfers between devices: 46 us -> 34.3 us  [local(): lax.all_gather(outer_weight, 'fsdp', axis=0, tiled=True)]
    reshape x0 -> x2, local copies, waits for them, and re-layouts: none -> 10.2 us  [the longest x1 6.23 us: local(): gathered_values.reshape(num_blocks, blk_size, HEADS, HEAD_DIM)]
    unnamed x144 -> x146, local copies, waits for them, and re-layouts: 30.2 us -> 39.5 us
    unnamed x12 -> x13, waiting for transfers between devices: 31 us -> 30.9 us
  transfers between devices with their start and end apart: 11 -> 12, of which waited for: 10 -> 10; matrix products, arithmetic and copies ran while one was open for 14% -> 18% of each run, Pallas kernels for 0% -> 0%
where the time goes in v1:
time: 962 us; the launch traced here: 953 us
  waiting for transfers between devices  447 us (46%)
  blocking collectives  198 us (21%)
  local copies, waits for them, and re-layouts  121 us (13%)
  matrix products  117 us (12%)
  other arithmetic  50.1 us (5%)
  between operations  17.1 us (2%)
    psum x1, blocking collectives, local(): lax.psum((qkv_part, qbias_part, vbias_part, proj_part, pbias_part, gain1_...  157 us
    reduce_scatter x1, waiting for transfers between devices, local(): lax.psum_scatter(terms.reshape(total_rows, 2 * feat_width), 'ctx', scatte...  115 us
    reduce_scatter x1, waiting for transfers between devices, local(): lax.psum_scatter(outer_grad.astype(jnp.bfloat16), 'fsdp', scatter_dimensi...  60.1 us
    reduce_scatter x1, waiting for transfers between devices, local(): lax.psum_scatter(inner_grad.astype(jnp.bfloat16), 'fsdp', scatter_dimensi...  59.9 us
    all_gather x1, waiting for transfers between devices, local(): lax.all_gather(jnp.concatenate([key_rows, value_rows], axis=1), 'ctx', ax...  50.2 us
    unnamed x146, local copies, waits for them, and re-layouts  39.5 us
    all_gather x1, waiting for transfers between devices, local(): lax.all_gather(outer_weight, 'fsdp', axis=0, tiled=True)  34.3 us
    unnamed x2, blocking collectives  33.4 us
  transfers between devices with their start and end apart: 12, of which 10 were waited for; matrix products, arithmetic and copies ran while one was open for 18% of the time, Pallas kernels for 0%

profile of v1, /device:TPU:0, one launch (start us, length us, event | category | flops | bytes accessed | tf_op | source)
XLA Modules:
  0.0 952.7 jit_solution(11985647301799897399)
XLA Ops:
  15.8 17.8 %all-reduce.19 = (bf16[768]{0:T(1024)(128)(2,1)S(1)}, bf16[768]{0:T(1024)(128)(2,1)S(1)}, bf16[768]{0:T(1024)(128)(2,1)S(1)}, bf16[768]{0:T(1024)(128)(2,1)S(1)}...) all-reduce(bf16[768]{0:T(1024)(128)(2,1)S(1)} %dynamic-update-slice, ...), channel_id=1, replica_groups=mesh['fsdp'=4,'ctx'=8] {'fsdp'}, use_global_device_ids=true, to_apply=%add.1 | all-reduce | flops 5376 | bytes 21504
  33.7 26.3 %all-gather.9.cloned.1.call-done = bf16[768,2304]{1,0:T(8,128)(2,1)} async-done(((bf16[192,2304]{1,0:T(8,128)(2,1)}), bf16[768,2304]{1,0:T(8,128)(2,1)}) %all-gather.9.cloned.1.call-update) | async-done | bytes 3538960 | tf_op jit(solution)/shard_map/all_gather | solution.py:80
  60.0 3.2 fusion.68
  69.0 8.1 all-gather
  80.3 22.3 %all-gather.19.cloned.1.call-done = bf16[2048,768]{1,0:T(8,128)(2,1)} async-done(((bf16[256,768]{1,0:T(8,128)(2,1)}), bf16[2048,768]{1,0:T(8,128)(2,1)}) %all-gather.19.cloned.1.call-update) | async-done | bytes 3145744 | tf_op jit(solution)/shard_map/all_gather | solution.py:191
  102.6 3.2 copy.90
  105.8 4.0 reshape.235
  109.8 3.1 copy.93
  112.9 29.1 %all-gather.21.cloned.1.call-done = bf16[2048,768]{1,0:T(8,128)(2,1)} async-done(((bf16[256,768]{1,0:T(8,128)(2,1)}), bf16[2048,768]{1,0:T(8,128)(2,1)}) %all-gather.21.cloned.1.call-update) | async-done | bytes 3145744 | tf_op jit(solution)/shard_map/all_gather | solution.py:192
  142.0 4.8 copy.91
  146.8 6.2 reshape.236
  153.1 4.5 copy.94
  157.6 50.2 %all-gather.11.cloned.1.call-done = bf16[2048,1536]{1,0:T(8,128)(2,1)} async-done(((bf16[256,1536]{1,0:T(8,128)(2,1)}), bf16[2048,1536]{1,0:T(8,128)(2,1)}) %all-gather.11.cloned.1.call-update) | async-done | bytes 6291472 | tf_op jit(solution)/shard_map/all_gather | solution.py:113
  207.8 5.9 fusion.98
  213.7 4.7 copy.85
  218.4 6.1 reshape.232
  224.5 4.5 copy.88
  229.1 4.8 copy.87
  233.8 6.1 reshape.234
  240.0 4.6 copy.89
  244.6 55.6 %while.32 = (s32[]{:T(128)}, f32[12,256]{1,0:T(8,128)S(1)}, f32[12,256]{1,0:T(8,128)}, f32[256,12,64]{0,2,1:T(8,128)}, s32[2]{0:T(128)}, /*index=5*/s32[16]{0:T(...) while((s32[]{:T(128)}, f32[12,256]{1,0:T(8,128)S(1)}, ...), condition=%wide.region_4.5_spmd.clone, body=%wide.region_0.4_spmd.clone.sunk | while | flops 840597504 | bytes 93516152 | solution.py:146
  248.7 9.4 bitcast_reduce_fusion.2
  258.9 7.4 fusion.157
  267.1 5.4 fusion.159
  276.5 9.4 bitcast_reduce_fusion.2
  286.7 7.4 fusion.157
  294.9 5.3 fusion.159
  300.2 2.0 fusion.84
  302.1 2.3 fusion.101
  306.9 12.4 %multiply_convert_fusion.1 = (bf16[256,3072]{1,0:T(8,128)(2,1)}, f32[256,3072]{1,0:T(8,128)}, f32[256,3072]{1,0:T(8,128)}) fusion(f32[3072]{0:T(1024)} %bitcast.173, bf16[768,3072]{1,0:T(8,128)(2,1)} %all-gather.15.cloned.1.call-done, f32[256,768]{1,0:T(8,128)} %copy-done.3, f32[768]{0:T(1024)} %convert_element_type.168, f32[768]{0:T(1024)} %convert_element_type.167, ...), kind=kOutput, calls=%fused_computation.91 | convolution fusion | flops 1260847104 | bytes 13389824 | tf_op jit(solution)/shard_map/dot_general | solution.py:160
  319.3 34.3 %all-gather.17.cloned.1.call-done = bf16[3072,768]{1,0:T(8,128)(2,1)} async-done(((bf16[768,768]{1,0:T(8,128)(2,1)}), bf16[3072,768]{1,0:T(8,128)(2,1)}) %all-gather.17.cloned.1.call-update) | async-done | bytes 4718608 | tf_op jit(solution)/shard_map/all_gather | solution.py:91
  353.6 4.7 fusion.102
  360.8 2.8 fusion.92
  363.6 2.4 multiply_reduce_fusion
  370.0 1.9 copy.92
  371.9 2.0 fusion.82
  373.9 81.6 %while.33 = (s32[]{:T(128)}, f32[256,12,64]{0,2,1:T(8,128)}, f32[2,1024,1536]{2,1,0:T(8,128)}, bf16[2,1024,12,64]{1,3,2,0:T(8,128)(2,1)S(1)}, s32[2]{0:T(128)}, ...) while((s32[]{:T(128)}, f32[256,12,64]{0,2,1:T(8,128)}, ...), condition=%wide.region_15.16_spmd.clone, body=%wide.region_13.15_spmd.clone.sunk | while | flops 2047752192 | bytes 193675104 | solution.py:232
  374.4 1.8 fusion.170
  379.2 6.4 multiply_convert_fusion.3
  385.6 5.0 fusion.172
  390.6 6.5 fusion.173
  397.1 2.0 convolution_multiply_fusion.2
  399.1 3.2 maximum_bitcast_fusion.2
  402.4 6.6 copy.124
  408.9 5.9 constant_dynamic-update-slice_fusion.2
  419.7 6.4 multiply_convert_fusion.3
  426.1 5.2 fusion.172
  431.2 6.5 fusion.173
  437.8 2.0 convolution_multiply_fusion.2
  439.8 3.2 maximum_bitcast_fusion.2
  443.0 6.6 copy.124
  449.6 5.9 constant_dynamic-update-slice_fusion.2
  458.3 3.9 convolution_convert_fusion.1
  464.0 3.6 convolution_convert_fusion
  469.9 115.1 %reduce-scatter.8.cloned.1.call-done = f32[256,1536]{1,0:T(8,128)} async-done(((f32[2048,1536]{1,0:T(8,128)}), f32[256,1536]{1,0:T(8,128)}) %reduce-scatter.8.cloned.1.call-update) | async-done | bytes 1572880 | tf_op jit(solution)/shard_map/reduce_scatter | solution.py:237
  587.3 2.2 fusion.67
  589.6 4.0 copy.107
  596.3 19.0 %reduce-scatter.10.cloned.1.call-done = bf16[192,768]{1,0:T(8,128)(2,1)} async-done(((bf16[768,768]{1,0:T(8,128)(2,1)}), bf16[192,768]{1,0:T(8,128)(2,1)}) %reduce-scatter.10.cloned.1.call-update) | async-done | bytes 294928 | tf_op jit(solution)/shard_map/reduce_scatter | solution.py:258
  615.4 59.9 %reduce-scatter.12.cloned.1.call-done = bf16[192,3072]{1,0:T(8,128)(2,1)} async-done(((bf16[768,3072]{1,0:T(8,128)(2,1)}), bf16[192,3072]{1,0:T(8,128)(2,1)}) %reduce-scatter.12.cloned.1.call-update) | async-done | bytes 1179664 | tf_op jit(solution)/shard_map/reduce_scatter | solution.py:272
  675.3 60.1 %reduce-scatter.14.cloned.1.call-done = bf16[768,768]{1,0:T(8,128)(2,1)} async-done(((bf16[3072,768]{1,0:T(8,128)(2,1)}), bf16[768,768]{1,0:T(8,128)(2,1)}) %reduce-scatter.14.cloned.1.call-update) | async-done | bytes 1179664 | tf_op jit(solution)/shard_map/reduce_scatter | solution.py:278
  735.6 15.6 %all-reduce.18 = (bf16[768]{0:T(1024)(128)(2,1)S(1)}, bf16[768]{0:T(1024)(128)(2,1)S(1)}, bf16[768]{0:T(1024)(128)(2,1)S(1)}, bf16[768]{0:T(1024)(128)(2,1)S(1)}...) all-reduce(bf16[768]{0:T(1024)(128)(2,1)S(1)} %dynamic-update-slice, ...), channel_id=1, replica_groups=mesh['fsdp'=4,'ctx'=8] {'fsdp'}, use_global_device_ids=true, to_apply=%add.7 | all-reduce | flops 9984 | bytes 39936
  754.2 4.0 fusion.77
  758.1 27.7 %reduce-scatter.16.cloned.1.call-done = bf16[192,2304]{1,0:T(8,128)(2,1)} async-done(((bf16[768,2304]{1,0:T(8,128)(2,1)}), bf16[192,2304]{1,0:T(8,128)(2,1)}) %reduce-scatter.16.cloned.1.call-update) | async-done | bytes 884752
  787.4 156.5 %all-reduce.21 = (f32[192,2304]{0,1:T(8,128)S(1)}, f32[192]{0:T(256)}, f32[192]{0:T(256)}, f32[192,768]{1,0:T(8,128)}, f32[192]{0:T(256)}, /*index=5*/f32[192]{0...) all-reduce(bf16[192,2304]{0,1:T(8,128)(2,1)S(1)} %copy.108, ...), channel_id=1, replica_groups=mesh['fsdp'=4,'ctx'=8] {'ctx'}, use_global_device_ids=true, to_apply=%region_18.19 | all-reduce | flops 1771776 | bytes 10635264 | tf_op jit(solution)/shard_map/psum | solution.py:291
  (305 shorter events, 61.0 us)
Async XLA Ops:
  7.2 52.8 %all-gather.9.cloned.1.call-start = ((), (), s32[]{:S(2)}) async-start(), calls=%async_computation.5 | async-start | bytes 4423680 | tf_op jit(solution)/shard_map/all_gather | solution.py:80
  7.9 94.7 %all-gather.19.cloned.1.call-start = ((), (), s32[]{:S(2)}) async-start(), calls=%async_computation.10 | async-start | bytes 3538944 | tf_op jit(solution)/shard_map/all_gather | solution.py:191
  64.2 4.9 copy-start.65
  64.2 77.8 %all-gather.21.cloned.1.call-start = ((), (), s32[]{:S(2)}) async-start(), calls=%async_computation.11 | async-start | bytes 3538944 | tf_op jit(solution)/shard_map/all_gather | solution.py:192
  64.9 142.8 %all-gather.11.cloned.1.call-start = ((), (), s32[]{:S(2)}) async-start(), calls=%async_computation.6 | async-start | bytes 7077888 | tf_op jit(solution)/shard_map/all_gather | solution.py:113
  65.9 236.2 %all-gather.13.cloned.1.call-start = ((), (), s32[]{:S(2)}) async-start(), calls=%async_computation.7 | async-start | bytes 1474560 | tf_op jit(solution)/shard_map/all_gather | solution.py:83
  66.5 240.3 %all-gather.15.cloned.1.call-start = ((), (), s32[]{:S(2)}) async-start(), calls=%async_computation.8 | async-start | bytes 5898240 | tf_op jit(solution)/shard_map/all_gather | solution.py:89
  67.1 286.5 %all-gather.17.cloned.1.call-start = ((), (), s32[]{:S(2)}) async-start(), calls=%async_computation.9 | async-start | bytes 5898240 | tf_op jit(solution)/shard_map/all_gather | solution.py:91
  67.8 517.1 %reduce-scatter.8.cloned.1.call-start = ((), (), s32[]{:S(2)}) async-start(), calls=%async_computation.12 | async-start | bytes 14155776 | tf_op jit(solution)/shard_map/reduce_scatter | solution.py:237
  248.7 9.4 copy-start.31
  258.9 7.4 copy-start.26
  258.9 8.2 copy-start
  258.9 8.2 copy-start.32
  266.3 6.2 copy-start.27
  276.5 9.4 copy-start.31
  286.6 7.4 copy-start.26
  286.7 8.2 copy-start
  286.7 8.2 copy-start.32
  294.1 6.1 copy-start.27
  306.8 46.8 %copy-start.33 = (f32[768]{0:T(1024)S(1)}, f32[768]{0:T(1024)}, u32[]{:S(2)}) copy-start(f32[768]{0:T(1024)} %convert_element_type.167) | copy-start | bytes 9220
  306.8 46.8 %copy-start.36 = (f32[768]{0:T(1024)S(1)}, f32[768]{0:T(1024)}, u32[]{:S(2)}) copy-start(f32[768]{0:T(1024)} %convert_element_type.168) | copy-start | bytes 9220
  306.8 46.8 %copy-start.44 = (f32[256]{0:T(256)S(1)}, f32[256]{0:T(256)}, u32[]{:S(2)}) copy-start(f32[256]{0:T(256)} %copy-done.43) | copy-start | bytes 3076
  306.8 46.8 %copy-start.52 = (f32[256]{0:T(256)S(1)}, f32[256]{0:T(256)}, u32[]{:S(2)}) copy-start(f32[256]{0:T(256)} %fusion.85) | copy-start | bytes 3076
  353.6 7.1 slice-start.4
  353.6 5.0 copy-start.10
  353.6 5.0 copy-start.38
  353.6 7.1 slice-start.5
  353.6 7.1 copy-start.69
  358.6 4.9 copy-start.50
  366.0 5.9 copy-start.29
  374.3 4.8 copy-start.15
  374.4 4.8 copy-start.22
  374.4 4.8 copy-start.47
  374.4 4.8 copy-start.48
  376.2 9.3 copy-start.1
  385.6 5.0 copy-start.23
  385.6 5.0 copy-start.49
  385.6 11.5 %slice-start = ((s8[6291456]{0:T(1024)(128)(4,1)}), s8[4194304]{0:T(1024)(128)(4,1)S(1)}, s32[]{:S(2)}) async-start(s8[6291456]{0:T(1024)(128)(4,1)} %bitcast.160), calls=%async_computation.17 | async-start | bytes 8388608 | tf_op jit(solution)/shard_map/while
  390.6 6.5 slice-start.1
  414.9 4.8 copy-start.47
  414.9 4.8 copy-start.48
  416.7 9.3 copy-start.1
  426.1 5.2 copy-start.23
  426.1 5.2 copy-start.49
  426.1 11.7 %slice-start = ((s8[6291456]{0:T(1024)(128)(4,1)}), s8[4194304]{0:T(1024)(128)(4,1)S(1)}, s32[]{:S(2)}) async-start(s8[6291456]{0:T(1024)(128)(4,1)} %bitcast.160), calls=%async_computation.17 | async-start | bytes 8388608 | tf_op jit(solution)/shard_map/while
  431.2 6.5 slice-start.1
  455.6 159.7 %reduce-scatter.10.cloned.1.call-start = ((), (), s32[]{:S(2)}) async-start(), calls=%async_computation.13 | async-start | bytes 1474560 | tf_op jit(solution)/shard_map/reduce_scatter | solution.py:258
  458.2 217.2 %reduce-scatter.12.cloned.1.call-start = ((), (), s32[]{:S(2)}) async-start(), calls=%async_computation.14 | async-start | bytes 5898240 | tf_op jit(solution)/shard_map/reduce_scatter | solution.py:272
  462.2 273.2 %reduce-scatter.14.cloned.1.call-start = ((), (), s32[]{:S(2)}) async-start(), calls=%async_computation.15 | async-start | bytes 5898240 | tf_op jit(solution)/shard_map/reduce_scatter | solution.py:278
  467.7 318.2 %reduce-scatter.16.cloned.1.call-start = ((), (), s32[]{:S(2)}) async-start(), calls=%async_computation.16 | async-start | bytes 4423680
  593.6 141.8 %copy-start.19 = (bf16[256,1536]{1,0:T(8,128)(2,1)S(1)}, bf16[256,1536]{1,0:T(8,128)(2,1)}, u32[]{:S(2)}) copy-start(bf16[256,1536]{1,0:T(8,128)(2,1)} %copy-done.18) | copy-start | bytes 2359300
  593.6 141.9 %copy-start.57 = (bf16[768]{0:T(1024)(128)(2,1)S(1)}, bf16[768]{0:T(1024)(128)(2,1)}, u32[]{:S(2)}) copy-start(bf16[768]{0:T(1024)(128)(2,1)} %get-tuple-element.562) | copy-start | bytes 4612
  593.6 141.9 %copy-start.58 = (bf16[768]{0:T(1024)(128)(2,1)S(1)}, bf16[768]{0:T(1024)(128)(2,1)}, u32[]{:S(2)}) copy-start(bf16[768]{0:T(1024)(128)(2,1)} %get-tuple-element.641) | copy-start | bytes 4612
  593.6 141.9 %copy-start.59 = (bf16[768]{0:T(1024)(128)(2,1)S(1)}, bf16[768]{0:T(1024)(128)(2,1)}, u32[]{:S(2)}) copy-start(bf16[768]{0:T(1024)(128)(2,1)} %get-tuple-element.645) | copy-start | bytes 4612
  593.6 141.9 %copy-start.60 = (bf16[3072]{0:T(1024)(128)(2,1)S(1)}, bf16[3072]{0:T(1024)(128)(2,1)}, u32[]{:S(2)}) copy-start(bf16[3072]{0:T(1024)(128)(2,1)} %get-tuple-element.643) | copy-start | bytes 18436
  593.6 141.9 %copy-start.63 = (bf16[768]{0:T(1024)(128)(2,1)S(1)}, bf16[768]{0:T(1024)(128)(2,1)}, u32[]{:S(2)}) copy-start(bf16[768]{0:T(1024)(128)(2,1)} %get-tuple-element.560) | copy-start | bytes 4612
  593.6 141.9 %copy-start.64 = (bf16[768]{0:T(1024)(128)(2,1)S(1)}, bf16[768]{0:T(1024)(128)(2,1)}, u32[]{:S(2)}) copy-start(bf16[768]{0:T(1024)(128)(2,1)} %get-tuple-element.564) | copy-start | bytes 4612
  593.7 159.6 %copy-start.7 = (f32[256,768]{1,0:T(8,128)S(1)}, f32[256,768]{1,0:T(8,128)}, u32[]{:S(2)}) copy-start(f32[256,768]{1,0:T(8,128)} %copy-done.6) | copy-start | bytes 2359300
  593.7 159.5 %copy-start.39 = (f32[768]{0:T(1024)S(1)}, f32[768]{0:T(1024)}, u32[]{:S(2)}) copy-start(f32[768]{0:T(1024)} %convert_element_type.173) | copy-start | bytes 9220
  593.7 159.5 %copy-start.42 = (f32[256]{0:T(256)S(1)}, f32[256]{0:T(256)}, u32[]{:S(2)}) copy-start(f32[256]{0:T(256)} %copy-done.41) | copy-start | bytes 3076
  593.7 159.5 %copy-start.51 = (f32[256]{0:T(256)S(1)}, f32[256]{0:T(256)}, u32[]{:S(2)}) copy-start(f32[256]{0:T(256)} %copy-done.50) | copy-start | bytes 3076
  593.7 160.5 %copy-start.17 = (f32[256,768]{1,0:T(8,128)S(1)}, f32[256,768]{1,0:T(8,128)}, u32[]{:S(2)}) copy-start(f32[256,768]{1,0:T(8,128)} %copy-done.16) | copy-start | bytes 2359300
  593.7 160.5 %copy-start.30 = (bf16[256,768]{1,0:T(8,128)(2,1)S(1)}, bf16[256,768]{1,0:T(8,128)(2,1)}, u32[]{:S(2)}) copy-start(bf16[256,768]{1,0:T(8,128)(2,1)} %copy.96) | copy-start | bytes 1179652
  593.7 160.5 %copy-start.62 = (f32[256]{0:T(256)S(1)}, f32[256]{0:T(256)}, u32[]{:S(2)}) copy-start(f32[256]{0:T(256)} %copy-done.61) | copy-start | bytes 3076
  (40 other events, 91.0 us)
Sparse Core Ops, SparseCore 0:
  9.9 50.0 all-gather.8
  64.3 38.2 all-gather.18
  104.8 37.1 all-gather.20
  144.1 63.6 all-gather.10
  209.4 26.3 all-gather.12
  237.5 57.0 all-gather.14
  296.5 57.0 all-gather.16
  455.7 129.2 reduce-scatter.7
  588.4 26.8 reduce-scatter.9
  618.2 57.0 reduce-scatter.11
  678.3 57.0 reduce-scatter.13
  738.4 47.4 reduce-scatter.15
